TPU v7x, 32 devices: a whole 2x2x4 slice. The times are simulated.
32 devices in a mesh: dp: 8 (over z, x), mp: 4 (over y, core).
Axes of the slice: x: 2, y: 2, z: 4, core: 2. Of those that a mesh axis runs over, the one named last changes fastest.
Arguments:
- tokens: bfloat16 [32768, 768], P(('dp', 'mp')), may hold values from -6 to 6
- segments: int32 [64, 512], P(('dp', 'mp')), may hold values from 0 to 5, never falling along the last dimension, each value on 1 to 256 neighbouring positions
- head_mask: int32 [12], replicated, may hold values 0 or 1
- unit_mask: int32 [3072], replicated, may hold values 0 or 1
- hidden_mask: int32 [768], replicated, may hold values 0 or 1
- layer_gates: float32 [2], replicated, may hold values from 0.5 to 1.5
- qkv_weight: bfloat16 [768, 2304], P('mp'), may hold values from -0.21875 to 0.21875
- out_weight: bfloat16 [768, 768], P('mp'), may hold values from -1.75 to 1.75
- norm_gain: float32 [768], replicated, may hold values from 0.5 to 1.5
- norm_bias: float32 [768], replicated, may hold values from -3 to 3
- up_weight: bfloat16 [768, 3072], P(None, 'mp'), may hold values from -0.21875 to 0.21875
- down_weight: bfloat16 [768, 3072], P(None, 'mp'), may hold values from -0.109375 to 0.109375
- cotangent: bfloat16 [32768, 768], P(('dp', 'mp')), may hold values from -6 to 6
- owner_slot: int32 [48], replicated, may hold values from 0 to 47, as said below
- master: float32 [48, 384, 384], P('dp', 'mp'), may hold values from -0.21875 to 0.21875
- left_stats: float32 [48, 384, 384], P('dp', 'mp'), may hold values from -12582912 to 50331648
- right_stats: float32 [48, 384, 384], P('dp', 'mp'), may hold values from -12582912 to 50331648
- left_root: float32 [48, 384, 384], P('dp', 'mp'), may hold values from -1 to 1
- right_root: float32 [48, 384, 384], P('dp'), may hold values from -1 to 1
Outputs:
- output: bfloat16 [32768, 768], P(('dp', 'mp'))
- input_grad: float32 [32768, 768], P(('dp', 'mp'))
- head_grad: float32 [12], replicated
- unit_grad: float32 [3072], replicated
- hidden_grad: float32 [768], replicated
- layer_grad: float32 [2], replicated
- norm_grad: float32 [2, 768], replicated
- norm_new: float32 [2, 768], replicated
- block_grad: float32 [48, 384, 384], P('dp', 'mp')
- left_new: float32 [48, 384, 384], P('dp', 'mp')
- right_new: float32 [48, 384, 384], P('dp', 'mp')
- weight_new: float32 [48, 384, 384], P('dp', 'mp')
- weight_copy: bfloat16 [48, 384, 384], P('dp', 'mp')
Inputs may be any that keep to these rules, and one draw needn't show every extreme that they name: `segments`: in every block of 512 positions the item numbers run from 0 to 5 and never fall; each item has 1 to 256 positions, and one item of each block has exactly 256. `owner_slot`: every slot number appears exactly once.
All inputs are finite; a program needn't handle non-finite values.
Results may differ from a plain program's by a relative error of at most 0.017.
Values may be sent and summed in bfloat16 or wider, within the bound.
A program may use at most 192 MiB of HBM per device.

v0:
```python
from functools import partial
import math
import jax
import jax.numpy as jnp
from jax import lax
from jax.sharding import PartitionSpec as P

FF = 3072
SB = 384
HIGH = lax.Precision.HIGHEST
BETA = 0.5
RATE = 0.5
EPS = 1e-12
MASKED = -1e30


def gelu_exact(values):
    return jax.nn.gelu(values, approximate=False)


def normalize(summed, gain_in, offset, hidden_gate):
    centre = summed - jnp.mean(summed, axis=-1, keepdims=True)
    spread = jnp.mean(centre * centre, axis=-1, keepdims=True)
    return (centre * lax.rsqrt(spread + EPS) * gain_in + offset) * hidden_gate


def split_heads(block_joined, head_count):
    pieces = block_joined.reshape(block_joined.shape[0], 3, head_count, -1)
    return (pieces[:, 0], pieces[:, 1], pieces[:, 2])


def masked_scores(queries, keys_in, labels, factor):
    scores = (
        jnp.einsum("qhd,khd->hqk", queries, keys_in, preferred_element_type=jnp.float32) * factor
    )
    allowed = labels[:, None] == labels[None, :]
    return jnp.where(allowed[None], scores, MASKED)


def attend_forward(packed, head_count, factor):
    block_joined, labels = packed
    queries, keys_in, values_in = split_heads(block_joined, head_count)
    scores = masked_scores(queries, keys_in, labels, factor)
    highest = jnp.max(scores, axis=-1, keepdims=True)
    raised = jnp.exp(scores - highest)
    totals = jnp.sum(raised, axis=-1, keepdims=True)
    weights_low = (raised / totals).astype(jnp.bfloat16)
    context = jnp.einsum("hqk,khd->qhd", weights_low, values_in, preferred_element_type=jnp.float32)
    return (context, (highest + jnp.log(totals))[:, :, 0])


def attend_backward(packed, head_count, factor):
    block_joined, log_totals, context_grad, labels = packed
    queries, keys_in, values_in = split_heads(block_joined, head_count)
    scores = masked_scores(queries, keys_in, labels, factor)
    weights_full = jnp.exp(scores - log_totals[:, :, None])
    weights_low = weights_full.astype(jnp.bfloat16)
    values_grad = jnp.einsum(
        "hqk,qhd->khd", weights_low, context_grad, preferred_element_type=jnp.float32
    )
    weights_grad = jnp.einsum(
        "qhd,khd->hqk", context_grad, values_in, preferred_element_type=jnp.float32
    )
    inner_sum = jnp.sum(weights_full * weights_grad, axis=-1, keepdims=True)
    scores_grad = (weights_full * (weights_grad - inner_sum)).astype(jnp.bfloat16)
    queries_grad = (
        jnp.einsum("hqk,khd->qhd", scores_grad, keys_in, preferred_element_type=jnp.float32)
        * factor
    )
    keys_grad = (
        jnp.einsum("hqk,qhd->khd", scores_grad, queries, preferred_element_type=jnp.float32)
        * factor
    )
    merged = jnp.concatenate([queries_grad, keys_grad, values_grad], axis=1)
    return merged.reshape(merged.shape[0], -1).astype(jnp.bfloat16)


def contract_rows(left, right):
    return lax.dot_general(
        left, right, (((0,), (0,)), ((), ())), preferred_element_type=jnp.float32
    )


def contract_cols(left, right):
    return lax.dot_general(
        left, right, (((1,), (1,)), ((), ())), preferred_element_type=jnp.float32
    )


def body(
    tokens,
    segments,
    head_mask,
    unit_mask,
    hidden_mask,
    layer_gates,
    qkv_weight,
    out_weight,
    norm_gain,
    norm_bias,
    up_weight,
    down_weight,
    cotangent,
    owner_slot,
    master,
    left_stats,
    right_stats,
    left_root,
    right_root,
):
    row_count = tokens.shape[0]
    width = tokens.shape[1]
    head_count = head_mask.shape[0]
    head_width = width // head_count
    block_rows = segments.shape[1]
    block_count = segments.shape[0]
    factor = 1.0 / math.sqrt(head_width)
    model_size = lax.axis_size("mp")
    share = FF // model_size
    part_rows = SB // model_size
    total_tokens = row_count * lax.axis_size("dp") * model_size
    head_gate = head_mask.astype(jnp.float32)
    unit_gate = unit_mask.astype(jnp.float32)
    hidden_gate = hidden_mask.astype(jnp.float32)
    inputs = tokens.astype(jnp.float32)
    back_full = cotangent.astype(jnp.float32)
    qkv_full, out_full, up_full, down_full = (
        lax.all_gather(qkv_weight, "mp", axis=0, tiled=True),
        lax.all_gather(out_weight, "mp", axis=0, tiled=True),
        lax.all_gather(up_weight, "mp", axis=1, tiled=True),
        lax.all_gather(down_weight, "mp", axis=1, tiled=True),
    )
    joined_qkv = jnp.dot(tokens, qkv_full, preferred_element_type=jnp.float32).astype(jnp.bfloat16)
    joined_blocks = joined_qkv.reshape(block_count, block_rows, 3 * width)
    context, log_totals = lax.map(
        partial(attend_forward, head_count=head_count, factor=factor), (joined_blocks, segments)
    )
    context = context.reshape(row_count, head_count, head_width)
    gated_low = (context * head_gate[None, :, None]).reshape(row_count, width).astype(jnp.bfloat16)
    attn_out = jnp.dot(gated_low, out_full, preferred_element_type=jnp.float32)
    summed = inputs + layer_gates[0] * attn_out
    hidden, norm_pull = jax.vjp(normalize, summed, norm_gain, norm_bias, hidden_gate)
    hidden_low = hidden.astype(jnp.bfloat16)
    pre_act = jnp.dot(hidden_low, up_full, preferred_element_type=jnp.float32)
    active, gelu_pull = jax.vjp(gelu_exact, pre_act)
    active_low = (active * unit_gate).astype(jnp.bfloat16)
    branch = contract_cols(active_low, down_full)
    output = (hidden + layer_gates[1] * branch).astype(jnp.bfloat16)
    back_rounded = (layer_gates[1] * back_full).astype(jnp.bfloat16)
    qkv_full, out_full, up_full, down_full = (
        lax.all_gather(qkv_weight, "mp", axis=0, tiled=True),
        lax.all_gather(out_weight, "mp", axis=0, tiled=True),
        lax.all_gather(up_weight, "mp", axis=1, tiled=True),
        lax.all_gather(down_weight, "mp", axis=1, tiled=True),
    )
    grad_active = jnp.dot(back_rounded, down_full, preferred_element_type=jnp.float32)
    unit_grad = jnp.sum(grad_active * active, axis=0)
    grad_inner = gelu_pull(grad_active * unit_gate)[0].astype(jnp.bfloat16)
    hidden_back = contract_cols(grad_inner, up_full)
    up_term = contract_rows(grad_inner, hidden_low)
    down_term = contract_rows(active_low, back_rounded)
    unit_local = (
        lax.psum_scatter(
            jnp.stack([up_term, down_term], axis=1).astype(jnp.bfloat16),
            "mp",
            scatter_dimension=0,
            tiled=True,
        )
        .astype(jnp.float32)
        .transpose(1, 2, 0)
    )
    summed_grad, gain_grad, bias_grad, mask_grad = norm_pull(back_full + hidden_back)
    layer_grad = jnp.stack([jnp.sum(summed_grad * attn_out), jnp.sum(back_full * branch)])
    out_back = (layer_gates[0] * summed_grad).astype(jnp.bfloat16)
    gated_grad = contract_cols(out_back, out_full).astype(jnp.bfloat16)
    gated_heads = gated_grad.reshape(row_count, head_count, head_width)
    head_grad = jnp.sum(context * gated_heads.astype(jnp.float32), axis=(0, 2))
    context_grad = gated_heads * head_mask.astype(jnp.bfloat16)[None, :, None]
    joined_grad = lax.map(
        partial(attend_backward, head_count=head_count, factor=factor),
        (
            joined_blocks,
            log_totals,
            context_grad.reshape(block_count, block_rows, head_count, head_width),
            segments,
        ),
    )
    joined_grad = joined_grad.reshape(row_count, 3 * width)
    input_grad = summed_grad + contract_cols(joined_grad, qkv_full)
    tiles = width // SB
    qkv_term = jnp.einsum(
        "tri,tcj->rcij",
        tokens.reshape(row_count, tiles, SB),
        joined_grad.reshape(row_count, 3 * tiles, SB),
        preferred_element_type=jnp.float32,
    )
    out_term = jnp.einsum(
        "tri,tcj->rcij",
        gated_low.reshape(row_count, tiles, SB),
        out_back.reshape(row_count, tiles, SB),
        preferred_element_type=jnp.float32,
    )
    attn_terms = jnp.concatenate(
        [
            qkv_term.reshape(-1, model_size, part_rows, SB),
            out_term.reshape(-1, model_size, part_rows, SB),
        ],
        axis=0,
    )
    attn_rows = (
        lax.psum_scatter(attn_terms.astype(jnp.bfloat16), "mp", scatter_dimension=1, tiled=True)
        .astype(jnp.float32)
        .reshape(-1, part_rows, SB)
    )
    unit_split = unit_local.reshape(2, tiles, model_size, part_rows, share)
    unit_rows = lax.all_to_all(
        unit_split.astype(jnp.bfloat16), "mp", split_axis=2, concat_axis=4, tiled=True
    ).astype(unit_split.dtype)
    unit_rows = (
        unit_rows.reshape(2, tiles, part_rows, FF // SB, SB)
        .transpose(0, 1, 3, 2, 4)
        .reshape(-1, part_rows, SB)
    )
    all_rows = jnp.concatenate([attn_rows, unit_rows], axis=0)
    slot_order = jnp.argsort(owner_slot)
    slotted = jnp.take(all_rows, slot_order, axis=0)
    owned = lax.psum_scatter(
        slotted.astype(jnp.bfloat16), "dp", scatter_dimension=0, tiled=True
    ).astype(jnp.float32)
    full_grad = lax.all_gather(owned.astype(jnp.bfloat16), "mp", axis=1, tiled=True).astype(
        owned.dtype
    )
    row_start = lax.axis_index("mp") * part_rows
    columns = lax.dynamic_slice_in_dim(full_grad, row_start, part_rows, 2)
    left_new = BETA * left_stats + (1.0 - BETA) * jnp.einsum(
        "srj,skj->srk", owned, full_grad, precision=HIGH
    )
    right_new = BETA * right_stats + (1.0 - BETA) * jnp.einsum(
        "sjr,sjk->srk", columns, full_grad, precision=HIGH
    )
    left_part = jnp.einsum("sri,sij->srj", left_root, full_grad, precision=HIGH)
    update = jnp.einsum("srj,sjk->srk", left_part, right_root, precision=HIGH)
    weight_new = master - RATE * update
    norm_grad = jnp.stack([gain_grad, bias_grad])
    norm_grad, mask_grad, head_grad, layer_grad, unit_grad = lax.psum(
        (norm_grad, mask_grad, head_grad, layer_grad, unit_grad), ("dp", "mp")
    )
    norm_new = jnp.stack([norm_gain, norm_bias]) - 0.2 / math.sqrt(total_tokens) * norm_grad
    return (
        output,
        input_grad,
        head_grad,
        unit_grad,
        mask_grad,
        layer_grad,
        norm_grad,
        norm_new,
        owned,
        left_new,
        right_new,
        weight_new,
        weight_new.astype(jnp.bfloat16),
    )


def solution(mesh):
    return jax.shard_map(
        body,
        mesh=mesh,
        in_specs=(
            P(("dp", "mp"), None),
            P(("dp", "mp"), None),
            P(),
            P(),
            P(),
            P(),
            P("mp", None),
            P("mp", None),
            P(),
            P(),
            P(None, "mp"),
            P(None, "mp"),
            P(("dp", "mp"), None),
            P(),
            P("dp", "mp", None),
            P("dp", "mp", None),
            P("dp", "mp", None),
            P("dp", "mp", None),
            P("dp", None, None),
        ),
        out_specs=(
            P(("dp", "mp"), None),
            P(("dp", "mp"), None),
            P(),
            P(),
            P(),
            P(),
            P(),
            P(),
            P("dp", "mp", None),
            P("dp", "mp", None),
            P("dp", "mp", None),
            P("dp", "mp", None),
            P("dp", "mp", None),
        ),
        check_vma=False,
    )
```

profile of v0, /device:TPU:0, one launch (start us, length us, event | category | flops | bytes accessed | tf_op | source)
XLA Modules:
  0.0 672.5 jit_solution(17716247387969877652)
XLA Ops:
  19.6 23.5 %all-gather.6.cloned.1.call-done = bf16[768,2304]{1,0:T(8,128)(2,1)} async-done(((bf16[192,2304]{1,0:T(8,128)(2,1)}), bf16[768,2304]{1,0:T(8,128)(2,1)}) %all-gather.6.cloned.1.call-update) | async-done | bytes 3538960 | tf_op jit(solution)/shard_map/all_gather | solution.py:128
  43.1 8.4 %convolution_convert_fusion = bf16[1024,2304]{1,0:T(8,128)(2,1)} fusion(bf16[1024,768]{1,0:T(8,128)(2,1)} %param.23, bf16[768,2304]{1,0:T(8,128)(2,1)} %all-gather.6.cloned.1.call-done), kind=kOutput, calls=%fused_computation.70 | convolution fusion | flops 3626237952 | bytes 9830400 | tf_op jit(solution)/shard_map/dot_general | solution.py:133
  51.5 6.9 %copy.84 = bf16[2,512,2304]{1,2,0:T(8,128)(2,1)} copy(bf16[2,512,2304]{2,1,0:T(8,128)(2,1)} %bitcast.203) | data formatting | bytes 9437184 | tf_op jit(solution)/shard_map/while | solution.py:135
  58.4 28.8 %while.22 = (s32[]{:T(128)}, f32[2,512,12,64]{1,3,2,0:T(8,128)}, f32[2,12,512]{2,1,0:T(8,128)}, bf16[2,512,2304]{1,2,0:T(8,128)(2,1)}, s32[2,512]{1,0:T(2,128)S(1)}, /*index=5*/s32[]{:T(128)}) while((s32[]{:T(128)}, f32[2,512,12,64]{1,3,2,0:T(8,128)}, f32[2,12,512]{2,1,0:T(8,128)}, bf16[2,512,2304]{1,2,0:T(8,128)(2,1)}, ...), condition=%wide.region_3.4_spmd, body=%wide.region_0.3_spmd.sunk | while | flops 843311104 | bytes 58145924 | solution.py:135
  110.5 12.1 %fusion.54 = f32[1024,3072]{1,0:T(8,128)} fusion(bf16[768,3072]{1,0:T(8,128)(2,1)} %all-gather.10.cloned.1.call-done, f32[1024,768]{0,1:T(8,128)} %copy-done.5, f32[768]{0:T(1024)S(1)} %copy-done.30, f32[768]{0:T(1024)} %param.32, f32[768]{0:T(1024)S(1)} %copy-done.27, f32[1024]{0:T(1024)S(1)} %fusion.52, f32[1024]{0:T(1024)S(1)} %broadcast_multiply_fusion.1), kind=kOutput, calls=%fused_computation.128 | convolution fusion | flops 4836556800 | bytes 20464640 | tf_op jit(solution)/shard_map/dot_general | solution.py:144
  122.6 17.5 %all-gather.12.cloned.1.call-done = bf16[768,3072]{1,0:T(8,128)(2,1)} async-done(((bf16[768,768]{1,0:T(8,128)(2,1)}), bf16[768,3072]{1,0:T(8,128)(2,1)}) %all-gather.12.cloned.1.call-update) | async-done | bytes 4718608 | tf_op jit(solution)/shard_map/all_gather | solution.py:131
  140.1 38.9 %multiply_reduce_fusion.1 = (f32[3072]{0:T(1024)}, f32[1024,3072]{1,0:T(8,128)}, f32[1024,3072]{1,0:T(8,128)}) fusion(f32[1024,3072]{1,0:T(8,128)} %fusion.54, bf16[768,3072]{1,0:T(8,128)(2,1)} %all-gather.12.cloned.1.call-done, bf16[1024,768]{0,1:T(8,128)(2,1)} %copy.87, f32[]{:T(128)} %bitcast.21), kind=kOutput, calls=%fused_computation.51 | convolution fusion | flops 5041812480 | bytes 44052484 | tf_op jit(solution)/shard_map/dot_general | solution.py:156
  179.1 16.6 %add_convert_fusion = (bf16[1024,3072]{1,0:T(8,128)(2,1)}, bf16[1024,3072]{1,0:T(8,128)(2,1)}) fusion(f32[1024,3072]{1,0:T(8,128)} %get-tuple-element.182, f32[1024,3072]{1,0:T(8,128)} %get-tuple-element.202, f32[1024,3072]{1,0:T(8,128)S(1)} %bitcast.193, f32[3072]{0:T(1024)S(1)} %copy-done.40), kind=kLoop, calls=%fused_computation.52 | loop fusion | flops 56623104 | bytes 50343936 | tf_op jit(solution)/shard_map/convert_element_type | solution.py:158
  195.8 10.6 %fusion.36 = bf16[3072,1,768]{2,0,1:T(8,128)(2,1)} fusion(bf16[1024,3072]{1,0:T(8,128)(2,1)} %get-tuple-element.191, f32[1024,768]{0,1:T(8,128)S(1)} %copy-done.6, f32[768]{0:T(1024)S(1)} %copy-done.31, f32[768]{0:T(1024)S(1)} %copy-done.35, f32[768]{0:T(1024)S(1)} %copy-done.28, f32[1024]{0:T(1024)S(1)} %copy-done.33, f32[1024]{0:T(1024)S(1)} %copy-done.26), kind=kOutput, calls=%fused_computation.80 | convolution fusion | flops 4838916096 | bytes 14173184 | tf_op jit(solution)/shard_map/dot_general | solution.py:79
  206.4 7.7 %fusion.37 = bf16[3072,1,768]{2,0,1:T(8,128)(2,1)} fusion(bf16[1024,3072]{1,0:T(8,128)(2,1)S(1)} %copy-done.13, bf16[1024,768]{0,1:T(8,128)(2,1)S(1)} %copy-done.17, f32[]{:T(128)} %bitcast.21), kind=kOutput, calls=%fused_computation.81 | convolution fusion | flops 4836556800 | bytes 12582916 | tf_op jit(solution)/shard_map/dot_general | solution.py:79
  214.1 8.2 %pad_maximum_fusion.1 = bf16[3072,2,768]{2,0,1:T(8,128)(2,1)} fusion(bf16[3072,1,768]{2,0,1:T(8,128)(2,1)} %fusion.37, bf16[3072,1,768]{2,0,1:T(8,128)(2,1)} %fusion.36), kind=kLoop, calls=%fused_computation.68 | loop fusion | flops 4718592 | bytes 18874368 | tf_op jit(solution)/shard_map/stack | solution.py:164
  222.5 8.7 %fusion.61 = f32[1024,768]{0,1:T(8,128)S(1)} fusion(bf16[1024,3072]{1,0:T(8,128)(2,1)} %get-tuple-element.192, bf16[768,3072]{1,0:T(8,128)(2,1)} %all-gather.12.cloned.1.call-done), kind=kOutput, calls=%fused_computation.134 | convolution fusion | flops 4831838208 | bytes 14155776 | tf_op jit(solution)/shard_map/dot_general | solution.py:85
  231.2 14.8 %multiply_reduce_fusion.2 = (f32[768]{0:T(1024)}, f32[1024]{0:T(1024)S(1)}, f32[768]{0:T(1024)}, f32[768]{0:T(1024)}, bf16[1024,768]{0,1:T(8,128)(2,1)}, /*index=5*/f32[]{:T(128)}, f32[1024,768]{0,1:T(8,128)S(1)}) fusion(f32[1024,768]{0,1:T(8,128)S(1)} %copy-done.7, f32[768]{0:T(1024)S(1)} %copy-done.31, f32[1024]{0:T(1024)S(1)} %copy-done.33, ...), kind=kOutput, calls=%fused_computation.87 | convolution fusion | flops 4848349184 | bytes 23623688 | tf_op jit(solution)/shard_map/dot_general | solution.py:85
  266.7 55.7 %while.23 = (s32[]{:T(128)}, bf16[2,512,2304]{1,2,0:T(8,128)(2,1)}, bf16[2,512,2304]{1,2,0:T(8,128)(2,1)}, s32[2,512]{1,0:T(2,128)S(1)}, f32[2,12,512]{2,1,0:T(8...) while((s32[]{:T(128)}, bf16[2,512,2304]{1,2,0:T(8,128)(2,1)}, bf16[2,512,2304]{1,2,0:T(8,128)(2,1)}, ...), condition=%wide.region_10.11_spmd, body=%wide.region_8.10_spmd.sunk | while | flops 2065033216 | bytes 142990544 | solution.py:179
  271.3 7.0 %multiply_reduce_fusion.10 = (f32[12,512]{1,0:T(8,128)S(1)}, f32[12,512,512]{1,2,0:T(8,128)}) fusion(f32[12,512,512]{1,2,0:T(8,128)S(1)} %fusion.106, f32[12,512]{1,0:T(8,128)S(1)} %dynamic-slice_bitcast_fusion.3, pred[512,512]{0,1:T(8,128)(4,1)S(1)} %broadcast_compare_fusion.5, bf16[512,3,12,64]{0,3,2,1:T(8,128)(2,1)S(1)} %bitcast.186, ...), kind=kOutput, calls=%fused_computation.19.clone.1 | convolution fusion | flops 418375680 | bytes 27058180 | tf_op jit(solution)/shard_map/while/body/eval_jaxpr/qhd,khd->hqk/dot_general | solution.py:61
  278.3 7.1 %multiply_convert_fusion.12 = bf16[12,512,512]{1,2,0:T(8,128)(2,1)S(1)} fusion(f32[12,512,512]{1,2,0:T(8,128)} %get-tuple-element.280, f32[12,512,512]{1,2,0:T(8,128)S(1)} %fusion.106, f32[12,512]{1,0:T(8,128)S(1)} %get-tuple-element.281, f32[12,512]{1,0:T(8,128)S(1)} %dynamic-slice_bitcast_fusion.3, pred[512,512]{0,1:T(8,128)(4,1)S(1)} %broadcast_compare_fusion.5), kind=kLoop, calls=%fused_computation.18.clone.1 | loop fusion | flops 18874368 | bytes 31768576 | tf_op jit(solution)/shard_map/while/body/eval_jaxpr/convert_element_type | solution.py:65
  298.9 7.0 %multiply_reduce_fusion.10 = (f32[12,512]{1,0:T(8,128)S(1)}, f32[12,512,512]{1,2,0:T(8,128)}) fusion(f32[12,512,512]{1,2,0:T(8,128)S(1)} %fusion.106, f32[12,512]{1,0:T(8,128)S(1)} %dynamic-slice_bitcast_fusion.3, pred[512,512]{0,1:T(8,128)(4,1)S(1)} %broadcast_compare_fusion.5, bf16[512,3,12,64]{0,3,2,1:T(8,128)(2,1)S(1)} %bitcast.186, ...), kind=kOutput, calls=%fused_computation.19.clone.1 | convolution fusion | flops 418375680 | bytes 27058180 | tf_op jit(solution)/shard_map/while/body/eval_jaxpr/qhd,khd->hqk/dot_general | solution.py:61
  305.9 7.1 %multiply_convert_fusion.12 = bf16[12,512,512]{1,2,0:T(8,128)(2,1)S(1)} fusion(f32[12,512,512]{1,2,0:T(8,128)} %get-tuple-element.280, f32[12,512,512]{1,2,0:T(8,128)S(1)} %fusion.106, f32[12,512]{1,0:T(8,128)S(1)} %get-tuple-element.281, f32[12,512]{1,0:T(8,128)S(1)} %dynamic-slice_bitcast_fusion.3, pred[512,512]{0,1:T(8,128)(4,1)S(1)} %broadcast_compare_fusion.5), kind=kLoop, calls=%fused_computation.18.clone.1 | loop fusion | flops 18874368 | bytes 31768576 | tf_op jit(solution)/shard_map/while/body/eval_jaxpr/convert_element_type | solution.py:65
  322.4 9.9 %copy.95 = bf16[2,512,2304]{1,0,2:T(2,128)(2,1)} copy(bf16[2,512,2304]{1,2,0:T(8,128)(2,1)} %get-tuple-element.76) | data formatting | bytes 9437184 | tf_op jit(solution)/shard_map/while | solution.py:179
  332.3 8.7 %reshape_reshape.3 = bf16[1024,6,384]{0,2,1:T(8,128)(2,1)} reshape(bf16[2,512,2304]{1,0,2:T(2,128)(2,1)} %copy.95) | data formatting | bytes 9437184 | tf_op jit(solution)/shard_map/reshape;reshape | solution.py:194
  369.6 103.6 %all-reduce.4.cloned.1.call-done = bf16[16,4,96,384]{3,2,1,0:T(8,128)(2,1)} async-done(((bf16[16,4,96,384]{3,2,1,0:T(8,128)(2,1)}), bf16[16,4,96,384]{3,2,1,0:T(8,128)(2,1)}) %all-reduce.4.cloned.1.call-update) | async-done | bytes 4718608
  500.7 79.4 %reduce-scatter.8.cloned.1.call-done = bf16[6,96,384]{2,1,0:T(8,128)(2,1)} async-done(((bf16[48,96,384]{2,1,0:T(8,128)(2,1)}), bf16[6,96,384]{2,1,0:T(8,128)(2,1)}) %reduce-scatter.8.cloned.1.call-update) | async-done | bytes 442384 | tf_op jit(solution)/shard_map/reduce_scatter | solution.py:227
  588.9 41.4 %all-reduce.1 = (f32[12]{0:T(128)}, f32[3072]{0:T(1024)}, f32[768]{0:T(1024)}, f32[2]{0:T(128)}, f32[2,768]{1,0:T(2,128)}) all-reduce(f32[12]{0:T(128)} %multiply_reduce_fusion.5, f32[3072]{0:T(1024)} %get-tuple-element.181, f32[768]{0:T(1024)} %get-tuple-element.152, ...), channel_id=1, replica_groups=mesh['dp'=8,'mp'=4] {'dp','mp'}, use_global_device_ids=true, to_apply=%region_12.13 | all-reduce | flops 5390 | bytes 43120 | tf_op jit(solution)/shard_map/psum | solution.py:245
  637.0 9.8 %add_add_fusion.1 = f32[1024,768]{0,1:T(8,128)} fusion(f32[1024,768]{0,1:T(8,128)} %copy-done.11, bf16[1024,2304]{1,0:T(8,128)(2,1)} %bitcast.202, bf16[768,2304]{1,0:T(8,128)(2,1)} %all-gather.6.cloned.1.call-done, f32[1024]{0:T(1024)S(1)} %copy-done.44), kind=kOutput, calls=%fused_computation.99 | convolution fusion | flops 3625451520 | bytes 14553088 | tf_op jit(solution)/shard_map/dot_general | solution.py:85
  (246 shorter events, 201.3 us)
Async XLA Ops:
  7.2 651.3 %copy-start = (f32[6,384,384]{2,1,0:T(8,128)S(1)}, f32[6,384,384]{2,1,0:T(8,128)}, u32[]{:S(2)}) copy-start(f32[6,384,384]{2,1,0:T(8,128)} %param.41) | copy-start | bytes 10616836
  7.2 35.9 %all-gather.6.cloned.1.call-start = ((), (), s32[]{:S(2)}) async-start(), calls=%async_computation.3 | async-start | bytes 4423680 | tf_op jit(solution)/shard_map/all_gather | solution.py:128
  7.9 93.2 %all-gather.8.cloned.1.call-start = ((), (), s32[]{:S(2)}) async-start(), calls=%async_computation.4 | async-start | bytes 1474560 | tf_op jit(solution)/shard_map/all_gather | solution.py:129
  8.7 101.8 %all-gather.10.cloned.1.call-start = ((), (), s32[]{:S(2)}) async-start(), calls=%async_computation.5 | async-start | bytes 5898240 | tf_op jit(solution)/shard_map/all_gather | solution.py:130
  9.4 130.7 %all-gather.12.cloned.1.call-start = ((), (), s32[]{:S(2)}) async-start(), calls=%async_computation.6 | async-start | bytes 5898240 | tf_op jit(solution)/shard_map/all_gather | solution.py:131
  10.0 344.0 %reduce-scatter.6.cloned.1.call-start = ((), (), s32[]{:S(2)}) async-start(), calls=%async_computation.7 | async-start | bytes 11796480 | tf_op jit(solution)/shard_map/reduce_scatter | solution.py:163
  107.9 14.7 %copy-start.25 = (f32[1024]{0:T(1024)}, f32[1024]{0:T(1024)S(1)}, u32[]{:S(2)}) copy-start(f32[1024]{0:T(1024)S(1)} %broadcast_multiply_fusion.1) | copy-start | bytes 12292
  140.1 38.9 %slice-start = ((s8[12582912]{0:T(1024)(128)(4,1)}), s8[4194304]{0:T(1024)(128)(4,1)S(1)}, s32[]{:S(2)}) async-start(s8[12582912]{0:T(1024)(128)(4,1)} %bitcast.192), calls=%async_computation.11 | async-start | bytes 8388608
  140.1 38.9 %slice-start.1 = ((s8[12582912]{0:T(1024)(128)(4,1)}), s8[4194304]{0:T(1024)(128)(4,1)S(1)}, s32[]{:S(2)}) async-start(s8[12582912]{0:T(1024)(128)(4,1)} %bitcast.192), calls=%async_computation.12 | async-start | bytes 8388608
  140.1 38.9 %slice-start.2 = ((s8[12582912]{0:T(1024)(128)(4,1)}), s8[4194304]{0:T(1024)(128)(4,1)S(1)}, s32[]{:S(2)}) async-start(s8[12582912]{0:T(1024)(128)(4,1)} %bitcast.192), calls=%async_computation.13 | async-start | bytes 8388608
  140.1 38.9 %copy-start.40 = (f32[3072]{0:T(1024)S(1)}, f32[3072]{0:T(1024)}, u32[]{:S(2)}) copy-start(f32[3072]{0:T(1024)} %convert_element_type.116) | copy-start | bytes 36868
  179.1 16.7 %copy-start.6 = (f32[1024,768]{0,1:T(8,128)S(1)}, f32[1024,768]{0,1:T(8,128)}, u32[]{:S(2)}) copy-start(f32[1024,768]{0,1:T(8,128)} %copy-done.5) | copy-start | bytes 9437188
  179.1 16.7 %copy-start.26 = (f32[1024]{0:T(1024)S(1)}, f32[1024]{0:T(1024)}, u32[]{:S(2)}) copy-start(f32[1024]{0:T(1024)} %copy-done.25) | copy-start | bytes 12292
  179.1 16.6 %copy-start.28 = (f32[768]{0:T(1024)S(1)}, f32[768]{0:T(1024)}, u32[]{:S(2)}) copy-start(f32[768]{0:T(1024)} %param.31) | copy-start | bytes 9220
  179.1 16.6 %copy-start.31 = (f32[768]{0:T(1024)S(1)}, f32[768]{0:T(1024)}, u32[]{:S(2)}) copy-start(f32[768]{0:T(1024)} %convert_element_type.114) | copy-start | bytes 9220
  179.1 16.6 %copy-start.33 = (f32[1024]{0:T(1024)S(1)}, f32[1024]{0:T(1024)}, u32[]{:S(2)}) copy-start(f32[1024]{0:T(1024)} %copy-done.32) | copy-start | bytes 12292
  179.1 16.6 %copy-start.35 = (f32[768]{0:T(1024)S(1)}, f32[768]{0:T(1024)}, u32[]{:S(2)}) copy-start(f32[768]{0:T(1024)} %param.32) | copy-start | bytes 9220
  222.4 250.8 %all-reduce.4.cloned.1.call-start = ((), (), s32[]{:S(2)}) async-start(), calls=%async_computation.10 | async-start | bytes 9437184
  231.2 14.8 %copy-start.42 = (f32[1024]{0:T(1024)S(1)}, f32[1024]{0:T(1024)}, u32[]{:S(2)}) copy-start(f32[1024]{0:T(1024)} %copy-done.41) | copy-start | bytes 12292
  362.2 114.0 %all-to-all-start = ((bf16[2,2,4,96,768]{4,3,1,0,2:T(8,128)(2,1)}), bf16[2,2,4,96,768]{4,3,1,0,2:T(8,128)(2,1)}, u32[]{:S(2)}, u32[]{:S(2)}) async-start(bf16[2,2,4,96,768]{4,3,1,0,2:T(8,128)(2,1)} %copy.103), calls=%async_computation.1 | async-start | bytes 4718592 | tf_op jit(solution)/shard_map/all_to_all | solution.py:216
  366.9 213.2 %reduce-scatter.8.cloned.1.call-start = ((), (), s32[]{:S(2)}) async-start(), calls=%async_computation.8 | async-start | bytes 3981312 | tf_op jit(solution)/shard_map/reduce_scatter | solution.py:227
  500.6 79.5 %copy-start.29 = (f32[768]{0:T(1024)S(1)}, f32[768]{0:T(1024)}, u32[]{:S(2)}) copy-start(f32[768]{0:T(1024)} %param.31) | copy-start | bytes 9220
  500.6 79.5 %copy-start.37 = (f32[768]{0:T(1024)S(1)}, f32[768]{0:T(1024)}, u32[]{:S(2)}) copy-start(f32[768]{0:T(1024)} %param.32) | copy-start | bytes 9220
  500.6 154.9 %all-gather.14.cloned.1.call-start = ((), (), s32[]{:S(2)}) async-start(), calls=%async_computation.9 | async-start | bytes 2211840 | tf_op jit(solution)/shard_map/all_gather | solution.py:230
  (47 other events, 216.3 us)
Sparse Core Ops, SparseCore 0:
  9.6 33.4 all-gather.5
  44.7 17.4 all-gather.7
  63.7 37.4 all-gather.9
  102.6 37.4 all-gather.11
  222.5 78.3 reduce-scatter.5
  354.1 119.0 all-reduce.3
  500.7 79.2 reduce-scatter.7
  581.6 20.8 all-gather.13
where the time goes:
time: 682 us; the launch traced here: 672 us
  waiting for transfers between devices  227 us (33%)
  matrix products  187 us (27%)
  local copies, waits for them, and re-layouts  117 us (17%)
  other arithmetic  80.2 us (12%)
  blocking collectives  41.4 us (6%)
  between operations  15 us (2%)
    unnamed x9, waiting for transfers between devices  106 us
    reduce_scatter x1, waiting for transfers between devices, body(): lax.psum_scatter(slotted.astype(jnp.bfloat16), 'dp', scatter_dimension=0,...  79.4 us
    psum x1, blocking collectives, body(): lax.psum((norm_grad, mask_grad, head_grad, layer_grad, unit_grad), ('dp',...  41.4 us
    dot_general x1, matrix products, body(): jnp.dot(back_rounded, down_full, preferred_element_type=jnp.float32)  38.9 us
    dot_general x4, matrix products, contract_cols(): lax.dot_general(left, right, (((1,), (1,)), ((), ())), preferred_element_...  35.9 us
    all_gather x1, waiting for transfers between devices, body(): lax.all_gather(qkv_weight, 'mp', axis=0, tiled=True)  23.5 us
    unnamed x106, local copies, waits for them, and re-layouts  22.4 us
    dot_general x2, matrix products, contract_rows(): lax.dot_general(left, right, (((0,), (0,)), ((), ())), preferred_element_...  18.3 us
  transfers between devices with their start and end apart: 9, of which 4 were waited for; matrix products, arithmetic and copies ran while one was open for 38% of the time, Pallas kernels for 0%

commit v1 on v0

--- a/solution.py
+++ b/solution.py
@@ -1,3 +1,4 @@
+import functools
 from functools import partial
 import math
 import jax
@@ -12,6 +13,31 @@
 RATE = 0.5
 EPS = 1e-12
 MASKED = -1e30
+
+
+def edit_chains_on(packet, axis_id):
+    u1 = lax.axis_size(axis_id)
+    near, answer, everything = (u1, lax.axis_index(axis_id), packet.shape[1])
+    trail = [(dd, (dd + 1) % near) for dd in range(near)]
+    gallery = [(dd, (dd - 1) % near) for dd in range(near)]
+    carry_out = jnp.zeros((*packet.shape[:1], near * everything, *packet.shape[2:]), packet.dtype)
+    carry_out = lax.dynamic_update_slice_in_dim(carry_out, packet, answer * everything, axis=1)
+    e_next = local_next = packet
+    last = near // 2
+    for num in [*range(1, last + 1)]:
+        e_next = lax.ppermute(e_next, axis_name=axis_id, perm=trail)
+        carry_out = lax.dynamic_update_slice_in_dim(
+            carry_out, e_next, (answer - num) % near * everything, axis=1
+        )
+        if num < near - last:
+            local_next = lax.ppermute(local_next, axis_name=axis_id, perm=gallery)
+            carry_out = lax.dynamic_update_slice_in_dim(
+                carry_out, local_next, (answer + num) % near * everything, axis=1
+            )
+    return carry_out
+
+
+link_bars = functools.partial(edit_chains_on, axis_id="mp")
 
 
 def gelu_exact(values):
@@ -128,7 +154,7 @@
         lax.all_gather(qkv_weight, "mp", axis=0, tiled=True),
         lax.all_gather(out_weight, "mp", axis=0, tiled=True),
         lax.all_gather(up_weight, "mp", axis=1, tiled=True),
-        lax.all_gather(down_weight, "mp", axis=1, tiled=True),
+        link_bars(down_weight),
     )
     joined_qkv = jnp.dot(tokens, qkv_full, preferred_element_type=jnp.float32).astype(jnp.bfloat16)
     joined_blocks = joined_qkv.reshape(block_count, block_rows, 3 * width)

time: 682 us -> 703 us (1.031)
  local copies, waits for them, and re-layouts: 117 us -> 132 us
  starting transfers between devices: 4.96 us -> 14.8 us
    ppermute x0 -> x3, waiting for transfers between devices: none -> 37.5 us  [the longest x2 37.5 us: edit_chains_on(): e_next = lax.ppermute(e_next, axis_name=axis_id, perm=trail)]
    all_gather x1, waiting for transfers between devices: 23.5 us -> 0.01 us  [body(): lax.all_gather(qkv_weight, 'mp', axis=0, tiled=True)]
    all_gather x1, waiting for transfers between devices: 17.5 us -> 2.47 us  [body(): lax.all_gather(down_weight, 'mp', axis=1, tiled=True)]
    ppermute x0 -> x3, starting transfers between devices: none -> 9.59 us  [the longest x2 7.56 us: edit_chains_on(): e_next = lax.ppermute(e_next, axis_name=axis_id, perm=trail)]
    dynamic_update_slice x0 -> x4, local copies, waits for them, and re-layouts: none -> 8.57 us  [the longest x2 4.91 us: edit_chains_on(): lax.dynamic_update_slice_in_dim(carry_out, e_next, (answer - num) % near...]
    unnamed x106 -> x110, local copies, waits for them, and re-layouts: 22.4 us -> 22.1 us
  transfers between devices with their start and end apart: 9 -> 12, of which waited for: 4 -> 4; matrix products, arithmetic and copies ran while one was open for 38% -> 38% of each run, Pallas kernels for 0% -> 0%
where the time goes in v1:
time: 703 us; the launch traced here: 692 us
  waiting for transfers between devices  225 us (32%)
  matrix products  184 us (26%)
  local copies, waits for them, and re-layouts  132 us (19%)
  other arithmetic  79.1 us (11%)
  blocking collectives  41.2 us (6%)
  between operations  15 us (2%)
  starting transfers between devices  14.8 us (2%)
    unnamed x9, waiting for transfers between devices  106 us
    reduce_scatter x1, waiting for transfers between devices, body(): lax.psum_scatter(slotted.astype(jnp.bfloat16), 'dp', scatter_dimension=0,...  79.2 us
    psum x1, blocking collectives, body(): lax.psum((norm_grad, mask_grad, head_grad, layer_grad, unit_grad), ('dp',...  41.2 us
    dot_general x1, matrix products, body(): jnp.dot(back_rounded, down_full, preferred_element_type=jnp.float32)  38.9 us
    ppermute x2, waiting for transfers between devices, edit_chains_on(): e_next = lax.ppermute(e_next, axis_name=axis_id, perm=trail)  37.5 us
    dot_general x4, matrix products, contract_cols(): lax.dot_general(left, right, (((1,), (1,)), ((), ())), preferred_element_...  35.9 us
    unnamed x110, local copies, waits for them, and re-layouts  22.1 us
    dot_general x2, matrix products, contract_rows(): lax.dot_general(left, right, (((0,), (0,)), ((), ())), preferred_element_...  19.1 us
  transfers between devices with their start and end apart: 12, of which 4 were waited for; matrix products, arithmetic and copies ran while one was open for 38% of the time, Pallas kernels for 0%

profile of v1, /device:TPU:0, one launch (start us, length us, event | category | flops | bytes accessed | tf_op | source)
XLA Modules:
  0.0 691.9 jit_solution(1472658092736024290)
XLA Ops:
  12.0 37.5 %collective-permute-done = bf16[768,768]{1,0:T(8,128)(2,1)} collective-permute-done((bf16[768,768]{1,0:T(8,128)(2,1)}, bf16[768,768]{1,0:T(8,128)(2,1)}, u32[]{:S(2)}, u32[]{:S(2)}) %collective-permute-start) | collective-permute-done | bytes 1179680 | tf_op jit(solution)/shard_map/ppermute | solution.py:28
  49.5 7.1 %collective-permute-start.2 = (bf16[768,768]{1,0:T(8,128)(2,1)}, bf16[768,768]{1,0:T(8,128)(2,1)}, u32[]{:S(2)}, u32[]{:S(2)}) collective-permute-start(bf16[768,768]{1,0:T(8,128)(2,1)} %collective-permute-done), channel_id=1, source_target_pairs={{0,1},{1,2},{2,3},{3,0},{4,5},{5,6},{6,7},{7,4},{8,9},{9,10},{10,1... | collective-permute-start | bytes 3538952 | tf_op jit(solution)/shard_map/ppermute | solution.py:28
  77.6 8.5 %convolution_convert_fusion = bf16[1024,2304]{1,0:T(8,128)(2,1)} fusion(bf16[1024,768]{1,0:T(8,128)(2,1)} %param.23, bf16[768,2304]{1,0:T(8,128)(2,1)} %all-gather.6.cloned.1.call-done), kind=kOutput, calls=%fused_computation.70 | convolution fusion | flops 3626237952 | bytes 9830400 | tf_op jit(solution)/shard_map/dot_general | solution.py:159
  86.1 6.8 copy.84
  92.8 28.7 %while.22 = (s32[]{:T(128)}, f32[2,512,12,64]{1,3,2,0:T(8,128)}, f32[2,12,512]{2,1,0:T(8,128)}, bf16[2,512,2304]{1,2,0:T(8,128)(2,1)}, s32[2,512]{1,0:T(2,128)S(1)}, /*index=5*/s32[]{:T(128)}) while((s32[]{:T(128)}, f32[2,512,12,64]{1,3,2,0:T(8,128)}, f32[2,12,512]{2,1,0:T(8,128)}, bf16[2,512,2304]{1,2,0:T(8,128)(2,1)}, ...), condition=%wide.region_3.4_spmd, body=%wide.region_0.3_spmd.sunk | while | flops 843311104 | bytes 58554572 | solution.py:161
  145.1 11.4 %fusion.54 = f32[1024,3072]{1,0:T(8,128)} fusion(bf16[768,3072]{1,0:T(8,128)(2,1)} %all-gather.10.cloned.1.call-done, f32[1024,768]{0,1:T(8,128)} %copy-done.5, f32[768]{0:T(1024)S(1)} %copy-done.33, f32[768]{0:T(1024)} %param.32, f32[768]{0:T(1024)S(1)} %copy-done.30, f32[1024]{0:T(1024)S(1)} %fusion.52, f32[1024]{0:T(1024)S(1)} %broadcast_multiply_fusion.1), kind=kOutput, calls=%fused_computation.132 | convolution fusion | flops 4836556800 | bytes 20464640 | tf_op jit(solution)/shard_map/dot_general | solution.py:170
  158.9 38.9 %multiply_reduce_fusion.1 = (f32[3072]{0:T(1024)}, f32[1024,3072]{1,0:T(8,128)}, f32[1024,3072]{1,0:T(8,128)}) fusion(f32[1024,3072]{1,0:T(8,128)} %fusion.54, bf16[768,3072]{1,0:T(8,128)(2,1)} %all-gather.12.cloned.1.call-done, bf16[1024,768]{0,1:T(8,128)(2,1)} %copy.87, f32[]{:T(128)} %bitcast.21), kind=kOutput, calls=%fused_computation.51 | convolution fusion | flops 5041812480 | bytes 44052484 | tf_op jit(solution)/shard_map/dot_general | solution.py:182
  197.9 16.6 %add_convert_fusion = (bf16[1024,3072]{1,0:T(8,128)(2,1)}, bf16[1024,3072]{1,0:T(8,128)(2,1)}) fusion(f32[1024,3072]{1,0:T(8,128)} %get-tuple-element.182, f32[1024,3072]{1,0:T(8,128)} %get-tuple-element.202, f32[1024,3072]{1,0:T(8,128)S(1)} %bitcast.193, f32[3072]{0:T(1024)S(1)} %copy-done.45), kind=kLoop, calls=%fused_computation.52 | loop fusion | flops 56623104 | bytes 50343936 | tf_op jit(solution)/shard_map/convert_element_type | solution.py:184
  214.6 11.0 %fusion.37 = bf16[3072,1,768]{2,0,1:T(8,128)(2,1)} fusion(bf16[1024,3072]{1,0:T(8,128)(2,1)} %get-tuple-element.192, bf16[1024,768]{0,1:T(8,128)(2,1)S(1)} %copy-done.19, f32[]{:T(128)} %bitcast.21), kind=kOutput, calls=%fused_computation.81 | convolution fusion | flops 4836556800 | bytes 12582916 | tf_op jit(solution)/shard_map/dot_general | solution.py:105
  225.6 8.1 %fusion.36 = bf16[3072,1,768]{2,0,1:T(8,128)(2,1)} fusion(bf16[1024,3072]{1,0:T(8,128)(2,1)S(1)} %copy-done.14, f32[1024,768]{0,1:T(8,128)S(1)} %copy-done.6, f32[768]{0:T(1024)S(1)} %copy-done.34, f32[768]{0:T(1024)S(1)} %copy-done.40, f32[768]{0:T(1024)S(1)} %copy-done.31, f32[1024]{0:T(1024)S(1)} %copy-done.36, f32[1024]{0:T(1024)S(1)} %copy-done.29), kind=kOutput, calls=%fused_computation.80 | convolution fusion | flops 4838916096 | bytes 14173184 | tf_op jit(solution)/shard_map/dot_general | solution.py:105
  233.7 8.2 %pad_maximum_fusion.1 = bf16[3072,2,768]{2,0,1:T(8,128)(2,1)} fusion(bf16[3072,1,768]{2,0,1:T(8,128)(2,1)} %fusion.37, bf16[3072,1,768]{2,0,1:T(8,128)(2,1)} %fusion.36), kind=kLoop, calls=%fused_computation.68 | loop fusion | flops 4718592 | bytes 18874368 | tf_op jit(solution)/shard_map/stack | solution.py:190
  242.1 9.0 %convert_add_fusion = f32[1024,768]{0,1:T(8,128)S(1)} fusion(bf16[1024,768]{0,1:T(8,128)(2,1)} %copy.87, bf16[1024,3072]{1,0:T(8,128)(2,1)} %get-tuple-element.191, bf16[768,3072]{1,0:T(8,128)(2,1)} %all-gather.10.cloned.1.call-done), kind=kOutput, calls=%fused_computation.75 | convolution fusion | flops 4833411072 | bytes 15728640 | tf_op jit(solution)/shard_map/dot_general | solution.py:111
  251.1 14.6 %multiply_reduce_fusion.2 = (f32[768]{0:T(1024)}, f32[1024]{0:T(1024)S(1)}, f32[768]{0:T(1024)}, f32[768]{0:T(1024)}, bf16[1024,768]{0,1:T(8,128)(2,1)}, /*index=5*/f32[]{:T(128)}) fusion(f32[1024,768]{0,1:T(8,128)S(1)} %convert_add_fusion, f32[1024,768]{0,1:T(8,128)S(1)} %copy-done.7, f32[768]{0:T(1024)S(1)} %copy-done.34, f32[1024]{0:T(1024)S(1)} %copy-done.36, ...), kind=kOutput, calls=%fused_computation.87 | convolution fusion | flops 4847563776 | bytes 20477960 | tf_op jit(solution)/shard_map/dot_general | solution.py:111
  289.4 55.0 %while.23 = (s32[]{:T(128)}, bf16[2,512,2304]{1,2,0:T(8,128)(2,1)}, bf16[2,512,2304]{1,2,0:T(8,128)(2,1)}, s32[2,512]{1,0:T(2,128)S(1)}, f32[2,12,512]{2,1,0:T(8...) while((s32[]{:T(128)}, bf16[2,512,2304]{1,2,0:T(8,128)(2,1)}, bf16[2,512,2304]{1,2,0:T(8,128)(2,1)}, ...), condition=%wide.region_10.11_spmd, body=%wide.region_8.10_spmd.sunk | while | flops 2065033216 | bytes 176027952 | solution.py:205
  296.7 7.1 %multiply_reduce_fusion.10 = (f32[12,512]{1,0:T(8,128)S(1)}, f32[12,512,512]{1,2,0:T(8,128)}) fusion(f32[12,512,512]{1,2,0:T(8,128)S(1)} %fusion.105, f32[12,512]{1,0:T(8,128)S(1)} %dynamic-slice_bitcast_fusion.3, pred[512,512]{0,1:T(8,128)(4,1)S(1)} %broadcast_compare_fusion.5, bf16[512,3,12,64]{0,3,2,1:T(8,128)(2,1)S(1)} %bitcast.186, ...), kind=kOutput, calls=%fused_computation.19.clone.1 | convolution fusion | flops 418375680 | bytes 27058180 | tf_op jit(solution)/shard_map/while/body/eval_jaxpr/qhd,khd->hqk/dot_general | solution.py:87
  303.8 7.2 %multiply_convert_fusion.12 = bf16[12,512,512]{1,2,0:T(8,128)(2,1)S(1)} fusion(f32[12,512,512]{1,2,0:T(8,128)} %get-tuple-element.279, f32[12,512,512]{1,2,0:T(8,128)S(1)} %fusion.105, f32[12,512]{1,0:T(8,128)S(1)} %get-tuple-element.280, f32[12,512]{1,0:T(8,128)S(1)} %dynamic-slice_bitcast_fusion.3, pred[512,512]{0,1:T(8,128)(4,1)S(1)} %broadcast_compare_fusion.5), kind=kLoop, calls=%fused_computation.18.clone.1 | loop fusion | flops 18874368 | bytes 31768576 | tf_op jit(solution)/shard_map/while/body/eval_jaxpr/convert_element_type | solution.py:91
  324.2 7.1 %multiply_reduce_fusion.10 = (f32[12,512]{1,0:T(8,128)S(1)}, f32[12,512,512]{1,2,0:T(8,128)}) fusion(f32[12,512,512]{1,2,0:T(8,128)S(1)} %fusion.105, f32[12,512]{1,0:T(8,128)S(1)} %dynamic-slice_bitcast_fusion.3, pred[512,512]{0,1:T(8,128)(4,1)S(1)} %broadcast_compare_fusion.5, bf16[512,3,12,64]{0,3,2,1:T(8,128)(2,1)S(1)} %bitcast.186, ...), kind=kOutput, calls=%fused_computation.19.clone.1 | convolution fusion | flops 418375680 | bytes 27058180 | tf_op jit(solution)/shard_map/while/body/eval_jaxpr/qhd,khd->hqk/dot_general | solution.py:87
  331.3 7.1 %multiply_convert_fusion.12 = bf16[12,512,512]{1,2,0:T(8,128)(2,1)S(1)} fusion(f32[12,512,512]{1,2,0:T(8,128)} %get-tuple-element.279, f32[12,512,512]{1,2,0:T(8,128)S(1)} %fusion.105, f32[12,512]{1,0:T(8,128)S(1)} %get-tuple-element.280, f32[12,512]{1,0:T(8,128)S(1)} %dynamic-slice_bitcast_fusion.3, pred[512,512]{0,1:T(8,128)(4,1)S(1)} %broadcast_compare_fusion.5), kind=kLoop, calls=%fused_computation.18.clone.1 | loop fusion | flops 18874368 | bytes 31768576 | tf_op jit(solution)/shard_map/while/body/eval_jaxpr/convert_element_type | solution.py:91
  344.3 10.1 %copy.95 = bf16[2,512,2304]{1,0,2:T(2,128)(2,1)} copy(bf16[2,512,2304]{1,2,0:T(8,128)(2,1)} %get-tuple-element.76) | data formatting | bytes 9437184 | tf_op jit(solution)/shard_map/while | solution.py:205
  354.4 8.7 %reshape_reshape.3 = bf16[1024,6,384]{0,2,1:T(8,128)(2,1)} reshape(bf16[2,512,2304]{1,0,2:T(2,128)(2,1)} %copy.95) | data formatting | bytes 9437184 | tf_op jit(solution)/shard_map/reshape;reshape | solution.py:220
  389.4 103.4 %all-reduce.4.cloned.1.call-done = bf16[16,4,96,384]{3,2,1,0:T(8,128)(2,1)} async-done(((bf16[16,4,96,384]{3,2,1,0:T(8,128)(2,1)}), bf16[16,4,96,384]{3,2,1,0:T(8,128)(2,1)}) %all-reduce.4.cloned.1.call-update) | async-done | bytes 4718608
  520.5 79.2 %reduce-scatter.8.cloned.1.call-done = bf16[6,96,384]{2,1,0:T(8,128)(2,1)} async-done(((bf16[48,96,384]{2,1,0:T(8,128)(2,1)}), bf16[6,96,384]{2,1,0:T(8,128)(2,1)}) %reduce-scatter.8.cloned.1.call-update) | async-done | bytes 442384 | tf_op jit(solution)/shard_map/reduce_scatter | solution.py:253
  608.6 41.2 %all-reduce.1 = (f32[12]{0:T(128)}, f32[3072]{0:T(1024)}, f32[768]{0:T(1024)}, f32[2]{0:T(128)}, f32[2,768]{1,0:T(2,128)}) all-reduce(f32[12]{0:T(128)} %multiply_reduce_fusion.5, f32[3072]{0:T(1024)} %get-tuple-element.181, f32[768]{0:T(1024)} %get-tuple-element.152, ...), channel_id=1, replica_groups=mesh['dp'=8,'mp'=4] {'dp','mp'}, use_global_device_ids=true, to_apply=%region_12.13 | all-reduce | flops 5390 | bytes 43120 | tf_op jit(solution)/shard_map/psum | solution.py:271
  659.0 9.8 %add_add_fusion.1 = f32[1024,768]{0,1:T(8,128)} fusion(f32[1024,768]{0,1:T(8,128)} %copy-done.12, bf16[1024,2304]{1,0:T(8,128)(2,1)} %bitcast.204, bf16[768,2304]{1,0:T(8,128)(2,1)} %all-gather.6.cloned.1.call-done, f32[1024]{0:T(1024)S(1)} %copy-done.49), kind=kOutput, calls=%fused_computation.99 | convolution fusion | flops 3625451520 | bytes 14553088 | tf_op jit(solution)/shard_map/dot_general | solution.py:111
  (283 shorter events, 217.4 us)
Async XLA Ops:
  7.2 670.7 %copy-start = (f32[6,384,384]{2,1,0:T(8,128)S(1)}, f32[6,384,384]{2,1,0:T(8,128)}, u32[]{:S(2)}) copy-start(f32[6,384,384]{2,1,0:T(8,128)} %param.41) | copy-start | bytes 10616836
  7.2 70.4 %all-gather.6.cloned.1.call-start = ((), (), s32[]{:S(2)}) async-start(), calls=%async_computation.3 | async-start | bytes 4423680 | tf_op jit(solution)/shard_map/all_gather | solution.py:154
  7.9 127.8 %all-gather.8.cloned.1.call-start = ((), (), s32[]{:S(2)}) async-start(), calls=%async_computation.4 | async-start | bytes 1474560 | tf_op jit(solution)/shard_map/all_gather | solution.py:155
  8.7 136.4 %all-gather.10.cloned.1.call-start = ((), (), s32[]{:S(2)}) async-start(), calls=%async_computation.5 | async-start | bytes 5898240 | tf_op jit(solution)/shard_map/all_gather | solution.py:156
  9.4 52.4 %copy-start.55 = (s32[12]{0:T(128)S(1)}, s32[12]{0:T(128)}, u32[]{:S(2)}) copy-start(s32[12]{0:T(128)} %param.25) | copy-start | bytes 148
  9.4 53.6 %copy-start.51 = (s32[768]{0:T(1024)S(1)}, s32[768]{0:T(1024)}, u32[]{:S(2)}) copy-start(s32[768]{0:T(1024)} %param.27) | copy-start | bytes 9220
  9.4 149.5 %all-gather.12.cloned.1.call-start = ((), (), s32[]{:S(2)}) async-start(), calls=%async_computation.6 | async-start | bytes 5898240 | tf_op jit(solution)/shard_map/all_gather | solution.py:180
  9.5 40.0 %collective-permute-start = (bf16[768,768]{1,0:T(8,128)(2,1)}, bf16[768,768]{1,0:T(8,128)(2,1)}, u32[]{:S(2)}, u32[]{:S(2)}) collective-permute-start(bf16[768,768]{1,0:T(8,128)(2,1)} %param.34), channel_id=1, source_target_pairs={{0,1},{1,2},{2,3},{3,0},{4,5},{5,6},{6,7},{7,4},{8,9},{9,10},{10,1... | collective-permute-start | bytes 3538952 | tf_op jit(solution)/shard_map/ppermute | solution.py:28
  10.0 62.7 %collective-permute-start.1 = (bf16[768,768]{1,0:T(8,128)(2,1)}, bf16[768,768]{1,0:T(8,128)(2,1)}, u32[]{:S(2)}, u32[]{:S(2)}) collective-permute-start(bf16[768,768]{1,0:T(8,128)(2,1)} %param.34), channel_id=1, source_target_pairs={{0,3},{1,0},{2,1},{3,2},{4,7},{5,4},{6,5},{7,6},{8,11},{9,8},{10,9... | collective-permute-start | bytes 3538952 | tf_op jit(solution)/shard_map/ppermute | solution.py:33
  49.5 25.7 %collective-permute-start.2 = (bf16[768,768]{1,0:T(8,128)(2,1)}, bf16[768,768]{1,0:T(8,128)(2,1)}, u32[]{:S(2)}, u32[]{:S(2)}) collective-permute-start(bf16[768,768]{1,0:T(8,128)(2,1)} %collective-permute-done), channel_id=1, source_target_pairs={{0,1},{1,2},{2,3},{3,0},{4,5},{5,6},{6,7},{7,4},{8,9},{9,10},{10,1... | collective-permute-start | bytes 3538952 | tf_op jit(solution)/shard_map/ppermute | solution.py:28
  56.5 317.2 %reduce-scatter.6.cloned.1.call-start = ((), (), s32[]{:S(2)}) async-start(), calls=%async_computation.7 | async-start | bytes 11796480 | tf_op jit(solution)/shard_map/reduce_scatter | solution.py:189
  142.4 14.0 %copy-start.28 = (f32[1024]{0:T(1024)}, f32[1024]{0:T(1024)S(1)}, u32[]{:S(2)}) copy-start(f32[1024]{0:T(1024)S(1)} %broadcast_multiply_fusion.1) | copy-start | bytes 12292
  158.9 38.9 %slice-start = ((s8[12582912]{0:T(1024)(128)(4,1)}), s8[4194304]{0:T(1024)(128)(4,1)S(1)}, s32[]{:S(2)}) async-start(s8[12582912]{0:T(1024)(128)(4,1)} %bitcast.192), calls=%async_computation.11 | async-start | bytes 8388608
  158.9 38.9 %slice-start.1 = ((s8[12582912]{0:T(1024)(128)(4,1)}), s8[4194304]{0:T(1024)(128)(4,1)S(1)}, s32[]{:S(2)}) async-start(s8[12582912]{0:T(1024)(128)(4,1)} %bitcast.192), calls=%async_computation.12 | async-start | bytes 8388608
  158.9 38.9 %slice-start.2 = ((s8[12582912]{0:T(1024)(128)(4,1)}), s8[4194304]{0:T(1024)(128)(4,1)S(1)}, s32[]{:S(2)}) async-start(s8[12582912]{0:T(1024)(128)(4,1)} %bitcast.192), calls=%async_computation.13 | async-start | bytes 8388608
  158.9 38.9 %copy-start.45 = (f32[3072]{0:T(1024)S(1)}, f32[3072]{0:T(1024)}, u32[]{:S(2)}) copy-start(f32[3072]{0:T(1024)} %convert_element_type.116) | copy-start | bytes 36868
  197.9 16.6 %copy-start.19 = (bf16[1024,768]{0,1:T(8,128)(2,1)S(1)}, bf16[1024,768]{0,1:T(8,128)(2,1)}, u32[]{:S(2)}) copy-start(bf16[1024,768]{0,1:T(8,128)(2,1)} %copy.87) | copy-start | bytes 4718596
  242.0 250.9 %all-reduce.4.cloned.1.call-start = ((), (), s32[]{:S(2)}) async-start(), calls=%async_computation.10 | async-start | bytes 9437184
  251.1 14.6 %copy-start.47 = (f32[1024]{0:T(1024)S(1)}, f32[1024]{0:T(1024)}, u32[]{:S(2)}) copy-start(f32[1024]{0:T(1024)} %copy-done.46) | copy-start | bytes 12292
  382.1 113.9 %all-to-all-start = ((bf16[2,2,4,96,768]{4,3,1,0,2:T(8,128)(2,1)}), bf16[2,2,4,96,768]{4,3,1,0,2:T(8,128)(2,1)}, u32[]{:S(2)}, u32[]{:S(2)}) async-start(bf16[2,2,4,96,768]{4,3,1,0,2:T(8,128)(2,1)} %copy.103), calls=%async_computation.1 | async-start | bytes 4718592 | tf_op jit(solution)/shard_map/all_to_all | solution.py:242
  386.7 213.0 %reduce-scatter.8.cloned.1.call-start = ((), (), s32[]{:S(2)}) async-start(), calls=%async_computation.8 | async-start | bytes 3981312 | tf_op jit(solution)/shard_map/reduce_scatter | solution.py:253
  520.2 79.5 %copy-start.42 = (f32[768]{0:T(1024)S(1)}, f32[768]{0:T(1024)}, u32[]{:S(2)}) copy-start(f32[768]{0:T(1024)} %param.32) | copy-start | bytes 9220
  520.2 79.6 %copy-start.32 = (f32[768]{0:T(1024)S(1)}, f32[768]{0:T(1024)}, u32[]{:S(2)}) copy-start(f32[768]{0:T(1024)} %param.31) | copy-start | bytes 9220
  520.2 154.8 %all-gather.14.cloned.1.call-start = ((), (), s32[]{:S(2)}) async-start(), calls=%async_computation.9 | async-start | bytes 2211840 | tf_op jit(solution)/shard_map/all_gather | solution.py:256
  (62 other events, 304.5 us)
Sparse Core Ops, SparseCore 0:
  9.6 51.3 all-gather.5
  62.5 17.7 all-gather.7
  81.9 38.0 all-gather.9
  121.4 37.4 all-gather.11
  242.1 78.4 reduce-scatter.5
  373.9 118.9 all-reduce.3
  520.3 79.3 reduce-scatter.7
  601.3 20.8 all-gather.13
